TPU v7x, 128 devices: a whole 4x4x4 slice. The times are simulated.
128 devices in a mesh: expert: 64 (over z_hi, x, y, core), tensor: 2 (over z_lo).
Axes of the slice: x: 4, y: 4, z: 4 (z_hi: 2, z_lo: 2; z = z_hi * 2 + z_lo), core: 2. Of those that a mesh axis runs over, the one named last changes fastest.
Arguments:
- tokens: bfloat16 [32768, 768], P('expert'), may hold values from -6 to 6
- routes: int32 [32768, 2], P('expert'), may hold values from 0 to 15, all different within a row; in each aligned block of 512 rows (0 to 511, 512 to 1023, ...) at most 80 rows name the same one
- gain_one: float32 [768], replicated, may hold values from 0.5 to 1.5
- w_query: bfloat16 [768, 768], P(None, 'tensor'), may hold values from -0.21875 to 0.21875
- w_key: bfloat16 [768, 768], P(None, 'tensor'), may hold values from -0.21875 to 0.21875
- w_value: bfloat16 [768, 768], P(None, 'tensor'), may hold values from -0.21875 to 0.21875
- w_output: bfloat16 [768, 768], P('tensor'), may hold values from -3 to 3
- gain_two: float32 [768], replicated, may hold values from 0.5 to 1.5
- w_router: bfloat16 [768, 16], replicated, may hold values from -0.15625 to 0.15625
- shared_gate: bfloat16 [768, 2048], P(None, 'tensor'), may hold values from -0.21875 to 0.21875
- shared_up: bfloat16 [768, 2048], P(None, 'tensor'), may hold values from -0.21875 to 0.21875
- shared_down: bfloat16 [2048, 768], P('tensor'), may hold values from -0.125 to 0.125
- expert_gate: bfloat16 [64, 768, 512], P('expert', None, 'tensor'), may hold values from -0.21875 to 0.21875
- expert_up: bfloat16 [64, 768, 512], P('expert', None, 'tensor'), may hold values from -0.21875 to 0.21875
- expert_down: bfloat16 [64, 512, 768], P('expert', 'tensor'), may hold values from -0.125 to 0.125
- cotangent: bfloat16 [32768, 768], P('expert'), may hold values from -6 to 6
Outputs:
- block_out: bfloat16 [32768, 768], P('expert')
- grad_tokens: float32 [32768, 768], P('expert')
- grad_gain_one: float32 [768], replicated
- grad_w_query: float32 [768, 768], P(None, 'tensor')
- grad_w_key: float32 [768, 768], P(None, 'tensor')
- grad_w_value: float32 [768, 768], P(None, 'tensor')
- grad_w_output: float32 [768, 768], P('tensor')
- grad_gain_two: float32 [768], replicated
- grad_router: float32 [768, 16], replicated
- grad_shared_gate: float32 [768, 2048], P(None, 'tensor')
- grad_shared_up: float32 [768, 2048], P(None, 'tensor')
- grad_shared_down: float32 [2048, 768], P('tensor')
- grad_expert_gate: float32 [64, 768, 512], P('expert', None, 'tensor')
- grad_expert_up: float32 [64, 768, 512], P('expert', None, 'tensor')
- grad_expert_down: float32 [64, 512, 768], P('expert', 'tensor')
Inputs may be any that keep to these rules, and one draw needn't show every extreme that they name: `routes`: in each device's block of 512 rows no expert is named by more than 80 rows, a bound that some block reaches; the 2 entries of a row differ, and every expert is named somewhere.
All inputs are finite; a program needn't handle non-finite values.
Results may differ from a plain program's by a relative error of at most 0.02.
Values may be sent and summed in bfloat16 or wider, within the bound.
No kernel may reach another device: no remote copies, remote signals or barrier semaphores. Data moves between devices by JAX's collectives and lax.ppermute only.
A program may use at most 256 MiB of HBM per device.

v0:
```python
import jax
import jax.numpy as jnp
from jax import lax
from jax.sharding import PartitionSpec as P

HEAD_DIM = 64
BLOCK = 256
SEQ_DEVS = 4


epsilon = 1e-06
rope_base = 10000.0
masked_out = -1e30
precise = lax.Precision.HIGHEST


def shifted(x, axis, by):
    peers = lax.axis_size(axis)
    pairs = [(i, i + by) for i in range(peers) if 0 <= i + by < peers]
    return lax.ppermute(x, axis, pairs)


def swish_unit(values):
    return values * jax.nn.sigmoid(values)


def swish_slope(values):
    sigmoid = jax.nn.sigmoid(values)
    return sigmoid * (1.0 + values * (1.0 - sigmoid))


def rms_scale(values):
    return lax.rsqrt(jnp.mean(values * values, axis=-1, keepdims=True) + epsilon)


def rotary(values, places, direction):
    midpoint = values.shape[-1] // 2
    frequency = rope_base ** (-jnp.arange(midpoint, dtype=jnp.float32) * 2.0 / values.shape[-1])
    angles = places.astype(jnp.float32)[:, None] * frequency[None, :]
    cosine = jnp.cos(angles)[:, None, :]
    sine_part = direction * jnp.sin(angles)[:, None, :]
    leading = values[..., :midpoint]
    trailing = values[..., midpoint:]
    return jnp.concatenate(
        [leading * cosine - trailing * sine_part, trailing * cosine + leading * sine_part], axis=-1
    )


def norm_back(inputs, row_scale, gain_row, upstream):
    unit_rows = inputs * row_scale
    gain_grad = jnp.sum(upstream * unit_rows, axis=0)
    scaled_grad = upstream * gain_row
    input_grad = row_scale * (
        scaled_grad - unit_rows * jnp.mean(scaled_grad * unit_rows, axis=-1, keepdims=True)
    )
    return (input_grad, gain_grad)


def tensor_sum(values):
    return lax.psum(values.astype(jnp.bfloat16), "tensor").astype(jnp.float32)


def to_owner(buffer, group):
    copies = jnp.repeat(buffer, group, axis=0)
    arrived = lax.all_to_all(copies, "expert", split_axis=0, concat_axis=0, tiled=True)
    return arrived.reshape(-1, buffer.shape[2])


def from_owner(partial_value, sources, capacity, experts):
    width = partial_value.shape[1]
    shaped = partial_value.reshape(sources, capacity, width)
    summed = lax.psum(shaped.astype(jnp.bfloat16), "tensor")
    returned = lax.all_to_all(summed, "expert", split_axis=0, concat_axis=0, tiled=True)
    grouped = returned.reshape(experts, sources // experts, capacity, width).astype(jnp.float32)
    return jnp.sum(grouped, axis=1).reshape(-1, width)


def local(
    tokens,
    routes,
    gain_one,
    w_query,
    w_key,
    w_value,
    w_output,
    gain_two,
    w_router,
    shared_gate,
    shared_up,
    shared_down,
    expert_gate,
    expert_up,
    expert_down,
    cotangent,
):
    tok_rows = tokens.shape[0]
    model_width = tokens.shape[1]
    heads_here = w_query.shape[1] // HEAD_DIM
    experts = w_router.shape[1]
    choices_per = routes.shape[1]
    sources = lax.axis_size("expert")
    group = sources // experts
    capacity = max(2, (5 * tok_rows * choices_per + 4 * experts - 1) // (4 * experts))
    seq_place = lax.axis_index("expert") % SEQ_DEVS
    places = seq_place * tok_rows + jnp.arange(tok_rows, dtype=jnp.int32)
    head_shape = (tok_rows, heads_here, HEAD_DIM)
    score_scale = HEAD_DIM ** (-0.5)
    stream = tokens.astype(jnp.float32)
    scale_one = rms_scale(stream)
    normed = (stream * scale_one * gain_one).astype(jnp.bfloat16)
    query_rot = rotary(
        jnp.dot(normed, w_query, preferred_element_type=jnp.float32).reshape(head_shape),
        places,
        1.0,
    ).astype(jnp.bfloat16)
    key_rot = rotary(
        jnp.dot(normed, w_key, preferred_element_type=jnp.float32).reshape(head_shape), places, 1.0
    ).astype(jnp.bfloat16)
    value_low = jnp.dot(normed, w_value, preferred_element_type=jnp.float32).astype(jnp.bfloat16)
    own_pair = jnp.stack([key_rot.reshape(tok_rows, -1), value_low])
    earlier = []
    for distance in range(SEQ_DEVS - 1, 0, -1):
        earlier.append(shifted(own_pair, "expert", distance))
    all_pairs = jnp.concatenate(earlier + [own_pair], axis=1)
    key_span = all_pairs.shape[1]
    all_keys = all_pairs[0].reshape(key_span, heads_here, HEAD_DIM)
    all_values = all_pairs[1].reshape(key_span, heads_here, HEAD_DIM)
    key_places = (seq_place - (SEQ_DEVS - 1)) * tok_rows + jnp.arange(key_span, dtype=jnp.int32)
    allowed = (key_places[None, :] >= 0) & (
        key_places[None, :] // BLOCK <= places[:, None] // BLOCK
    )

    def scores_of():
        raw_scores = jnp.einsum(
            "qhd,khd->hqk", query_rot, all_keys, preferred_element_type=jnp.float32
        )
        return jnp.where(allowed[None], raw_scores * score_scale, masked_out)

    scores = scores_of()
    highest = jnp.max(scores, axis=-1, keepdims=True)
    weights = jnp.exp(scores - highest)
    weight_sum = jnp.sum(weights, axis=-1, keepdims=True)
    attention = weights / weight_sum
    log_total = highest + jnp.log(weight_sum)
    mixed_heads = (
        jnp.einsum(
            "hqk,khd->qhd",
            attention.astype(jnp.bfloat16),
            all_values,
            preferred_element_type=jnp.float32,
        )
        .astype(jnp.bfloat16)
        .reshape(tok_rows, -1)
    )
    middle = stream + tensor_sum(jnp.dot(mixed_heads, w_output, preferred_element_type=jnp.float32))
    scale_two = rms_scale(middle)
    normed_two = (middle * scale_two * gain_two).astype(jnp.bfloat16)
    logits = jnp.dot(normed_two, w_router, preferred_element_type=jnp.float32)
    choose = routes[:, :, None] == jnp.arange(experts, dtype=jnp.int32)[None, None, :]
    chosen = jnp.sum(jnp.where(choose, logits[:, None, :], 0.0), axis=-1)
    gate_weights = jnp.exp(chosen - jnp.max(chosen, axis=1, keepdims=True))
    gate_share = gate_weights / jnp.sum(gate_weights, axis=1, keepdims=True)
    gate_shared = jnp.dot(normed_two, shared_gate, preferred_element_type=jnp.float32)
    up_shared = jnp.dot(normed_two, shared_up, preferred_element_type=jnp.float32)
    hidden_shared = (swish_unit(gate_shared) * up_shared).astype(jnp.bfloat16)
    shared_out = tensor_sum(jnp.dot(hidden_shared, shared_down, preferred_element_type=jnp.float32))
    flat_routes = routes.reshape(-1)
    matches = (flat_routes[:, None] == jnp.arange(experts, dtype=jnp.int32)[None, :]).astype(
        jnp.int32
    )
    before = jnp.cumsum(matches, axis=0) - matches
    slot_index = jnp.sum(before * matches, axis=-1)
    targets = flat_routes * capacity + slot_index
    placer = (
        (targets[:, None] == jnp.arange(experts * capacity, dtype=jnp.int32)[None, :])
        .astype(jnp.bfloat16)
        .reshape(tok_rows, choices_per, experts * capacity)
    )
    placer_wide = placer.astype(jnp.float32)
    buffer = jnp.einsum(
        "tks,td->sd", placer, normed_two, preferred_element_type=jnp.float32
    ).astype(jnp.bfloat16)
    rows_in = to_owner(buffer.reshape(experts, capacity, model_width), group)
    gate_expert = jnp.dot(rows_in, expert_gate[0], preferred_element_type=jnp.float32)
    up_expert = jnp.dot(rows_in, expert_up[0], preferred_element_type=jnp.float32)
    hidden_expert = (swish_unit(gate_expert) * up_expert).astype(jnp.bfloat16)
    expert_out = from_owner(
        jnp.dot(hidden_expert, expert_down[0], preferred_element_type=jnp.float32),
        sources,
        capacity,
        experts,
    )
    picked = jnp.einsum(
        "tks,sd->tkd",
        placer_wide,
        expert_out,
        precision=precise,
        preferred_element_type=jnp.float32,
    )
    routed = jnp.sum(gate_share[:, :, None] * picked, axis=1)
    block_out = (middle + shared_out + routed).astype(jnp.bfloat16)
    grad_result = cotangent.astype(jnp.float32)
    gate_grads = jnp.sum(grad_result[:, None, :] * picked, axis=-1)
    out_grads = (gate_share[:, :, None] * grad_result[:, None, :]).astype(jnp.bfloat16)
    back_buffer = jnp.einsum(
        "tks,tkd->sd", placer, out_grads, preferred_element_type=jnp.float32
    ).astype(jnp.bfloat16)
    arrived_grads = to_owner(back_buffer.reshape(experts, capacity, model_width), group)
    hidden_grads = jnp.einsum(
        "rd,fd->rf", arrived_grads, expert_down[0], preferred_element_type=jnp.float32
    )
    grad_expert_down = jnp.einsum(
        "rf,rd->fd", hidden_expert, arrived_grads, preferred_element_type=jnp.float32
    )[None]
    expert_gate_grads = (hidden_grads * up_expert * swish_slope(gate_expert)).astype(jnp.bfloat16)
    expert_up_grads = (hidden_grads * swish_unit(gate_expert)).astype(jnp.bfloat16)
    grad_expert_gate = jnp.einsum(
        "rd,rf->df", rows_in, expert_gate_grads, preferred_element_type=jnp.float32
    )[None]
    grad_expert_up = jnp.einsum(
        "rd,rf->df", rows_in, expert_up_grads, preferred_element_type=jnp.float32
    )[None]
    rows_part = jnp.einsum(
        "rf,df->rd", expert_gate_grads, expert_gate[0], preferred_element_type=jnp.float32
    )
    rows_part = rows_part + jnp.einsum(
        "rf,df->rd", expert_up_grads, expert_up[0], preferred_element_type=jnp.float32
    )
    rows_grads = from_owner(rows_part, sources, capacity, experts)
    routed_grads = jnp.einsum(
        "tks,sd->td", placer_wide, rows_grads, precision=precise, preferred_element_type=jnp.float32
    )
    weighted = jnp.sum(gate_share * gate_grads, axis=1, keepdims=True)
    chosen_grads = gate_share * (gate_grads - weighted)
    logits_grads = jnp.sum(jnp.where(choose, chosen_grads[:, :, None], 0.0), axis=1).astype(
        jnp.bfloat16
    )
    grad_router = jnp.einsum(
        "td,te->de", normed_two, logits_grads, preferred_element_type=jnp.float32
    )
    router_back = jnp.einsum(
        "te,de->td", logits_grads, w_router, preferred_element_type=jnp.float32
    )
    result_low = grad_result.astype(jnp.bfloat16)
    grad_shared_down = jnp.einsum(
        "ts,td->sd", hidden_shared, result_low, preferred_element_type=jnp.float32
    )
    shared_hidden_grads = jnp.einsum(
        "td,sd->ts", result_low, shared_down, preferred_element_type=jnp.float32
    )
    shared_gate_grads = (shared_hidden_grads * up_shared * swish_slope(gate_shared)).astype(
        jnp.bfloat16
    )
    shared_up_grads = (shared_hidden_grads * swish_unit(gate_shared)).astype(jnp.bfloat16)
    grad_shared_gate = jnp.einsum(
        "td,ts->ds", normed_two, shared_gate_grads, preferred_element_type=jnp.float32
    )
    grad_shared_up = jnp.einsum(
        "td,ts->ds", normed_two, shared_up_grads, preferred_element_type=jnp.float32
    )
    shared_back = jnp.einsum(
        "ts,ds->td", shared_gate_grads, shared_gate, preferred_element_type=jnp.float32
    )
    shared_back = shared_back + jnp.einsum(
        "ts,ds->td", shared_up_grads, shared_up, preferred_element_type=jnp.float32
    )
    normed_two_grads = tensor_sum(shared_back) + router_back + routed_grads
    norm_part, grad_gain_two = norm_back(middle, scale_two, gain_two, normed_two_grads)
    middle_grads = grad_result + norm_part
    middle_low = middle_grads.astype(jnp.bfloat16)
    grad_w_output = jnp.einsum(
        "tc,td->cd", mixed_heads, middle_low, preferred_element_type=jnp.float32
    )
    mixed_grads = (
        jnp.einsum("td,cd->tc", middle_low, w_output, preferred_element_type=jnp.float32)
        .astype(jnp.bfloat16)
        .reshape(head_shape)
    )
    attention = jnp.exp(scores_of() - log_total)
    prob_grads = jnp.einsum(
        "qhd,khd->hqk", mixed_grads, all_values, preferred_element_type=jnp.float32
    )
    value_full = jnp.einsum(
        "hqk,qhd->khd",
        attention.astype(jnp.bfloat16),
        mixed_grads,
        preferred_element_type=jnp.float32,
    )
    score_grads = (
        attention
        * (prob_grads - jnp.sum(prob_grads * attention, axis=-1, keepdims=True))
        * score_scale
    ).astype(jnp.bfloat16)
    query_full = jnp.einsum(
        "hqk,khd->qhd", score_grads, all_keys, preferred_element_type=jnp.float32
    )
    key_full = jnp.einsum(
        "hqk,qhd->khd", score_grads, query_rot, preferred_element_type=jnp.float32
    )
    pair_grads = jnp.stack([key_full.reshape(key_span, -1), value_full.reshape(key_span, -1)])
    own_grads = pair_grads[:, (SEQ_DEVS - 1) * tok_rows :]
    for distance in range(1, SEQ_DEVS):
        offset = (SEQ_DEVS - 1 - distance) * tok_rows
        own_grads = own_grads + shifted(
            pair_grads[:, offset : offset + tok_rows].astype(jnp.bfloat16), "expert", -distance
        ).astype(jnp.float32)
    query_grads = rotary(query_full, places, -1.0).reshape(tok_rows, -1).astype(jnp.bfloat16)
    key_grads = (
        rotary(own_grads[0].reshape(head_shape), places, -1.0)
        .reshape(tok_rows, -1)
        .astype(jnp.bfloat16)
    )
    value_grads = own_grads[1].astype(jnp.bfloat16)
    grad_w_query = jnp.einsum("td,tc->dc", normed, query_grads, preferred_element_type=jnp.float32)
    grad_w_key = jnp.einsum("td,tc->dc", normed, key_grads, preferred_element_type=jnp.float32)
    grad_w_value = jnp.einsum("td,tc->dc", normed, value_grads, preferred_element_type=jnp.float32)
    normed_part = jnp.einsum("tc,dc->td", query_grads, w_query, preferred_element_type=jnp.float32)
    normed_part = normed_part + jnp.einsum(
        "tc,dc->td", key_grads, w_key, preferred_element_type=jnp.float32
    )
    normed_part = normed_part + jnp.einsum(
        "tc,dc->td", value_grads, w_value, preferred_element_type=jnp.float32
    )
    normed_grads = tensor_sum(normed_part)
    norm_first, grad_gain_one = norm_back(stream, scale_one, gain_one, normed_grads)
    grad_tokens = middle_grads + norm_first
    (
        grad_w_query,
        grad_w_key,
        grad_w_value,
        grad_w_output,
        grad_gain_one,
        grad_shared_gate,
        grad_shared_up,
        grad_shared_down,
        grad_router,
        grad_gain_two,
    ) = lax.psum(
        (
            grad_w_query,
            grad_w_key,
            grad_w_value,
            grad_w_output,
            grad_gain_one,
            grad_shared_gate,
            grad_shared_up,
            grad_shared_down,
            grad_router,
            grad_gain_two,
        ),
        "expert",
    )
    return (
        block_out,
        grad_tokens,
        grad_gain_one,
        grad_w_query,
        grad_w_key,
        grad_w_value,
        grad_w_output,
        grad_gain_two,
        grad_router,
        grad_shared_gate,
        grad_shared_up,
        grad_shared_down,
        grad_expert_gate,
        grad_expert_up,
        grad_expert_down,
    )


def solution(mesh):
    placed = (
        P("expert", None),
        P("expert", None),
        P(),
        P(None, "tensor"),
        P(None, "tensor"),
        P(None, "tensor"),
        P("tensor", None),
        P(),
        P(),
        P(None, "tensor"),
        P(None, "tensor"),
        P("tensor", None),
        P("expert", None, "tensor"),
        P("expert", None, "tensor"),
        P("expert", "tensor", None),
        P("expert", None),
    )
    return jax.shard_map(
        local,
        mesh=mesh,
        in_specs=placed,
        out_specs=(
            P("expert", None),
            P("expert", None),
            P(),
            P(None, "tensor"),
            P(None, "tensor"),
            P(None, "tensor"),
            P("tensor", None),
            P(),
            P(),
            P(None, "tensor"),
            P(None, "tensor"),
            P("tensor", None),
            P("expert", None, "tensor"),
            P("expert", None, "tensor"),
            P("expert", "tensor", None),
        ),
        check_vma=False,
    )
```

profile of v0, /device:TPU:1, one launch (start us, length us, event | category | flops | bytes accessed | tf_op | source)
XLA Modules:
  0.0 1993.8 jit_solution(18264545874733018892)
XLA Ops:
  31.4 5.8 collective-permute-done.2
  37.2 16.9 collective-permute-done.1
  54.1 11.0 collective-permute-done
  76.5 14.3 fusion.3
  90.8 12.0 fusion.2
  102.9 11.8 fusion.64
  125.2 45.2 %all-reduce.9.cloned.1.call-done = bf16[512,768]{1,0:T(8,128)(2,1)} async-done(((bf16[512,768]{1,0:T(8,128)(2,1)}), bf16[512,768]{1,0:T(8,128)(2,1)}) %all-reduce.9.cloned.1.call-update) | async-done | bytes 786448 | tf_op jit(solution)/shard_map/psum | solution.py:60
  178.4 10.5 all-to-all-start
  197.0 90.2 %all-to-all-done = bf16[64,80,768]{2,1,0:T(8,128)(2,1)} async-done(((bf16[64,80,768]{2,1,0:T(8,128)(2,1)}), bf16[64,80,768]{2,1,0:T(8,128)(2,1)}, u32[]{:S(2)}, u32[]{:S(2)}) %all-to-all-start) | async-done | bytes 7864352 | tf_op jit(solution)/shard_map/all_to_all | solution.py:65
  292.5 25.7 %all-to-all-start.2 = ((bf16[64,80,768]{2,1,0:T(8,128)(2,1)}), bf16[64,80,768]{2,1,0:T(8,128)(2,1)}, u32[]{:S(2)}, u32[]{:S(2)}) async-start(bf16[64,80,768]{2,1,0:T(8,128)(2,1)} %bitcast.155), calls=%async_computation.2 | async-start | bytes 15728640 | tf_op jit(solution)/shard_map/all_to_all | solution.py:65
  328.1 7.8 fusion.71
  336.0 7.9 fusion.75
  343.9 72.7 %all-to-all-done.2 = bf16[64,80,768]{2,1,0:T(8,128)(2,1)} async-done(((bf16[64,80,768]{2,1,0:T(8,128)(2,1)}), bf16[64,80,768]{2,1,0:T(8,128)(2,1)}, u32[]{:S(2)}, u32[]{:S(2)}) %all-to-all-start.2) | async-done | bytes 7864352 | tf_op jit(solution)/shard_map/all_to_all | solution.py:65
  416.5 9.9 multiply_convert_fusion.1
  431.9 7.6 fusion.73
  439.5 10.8 add_convert_fusion
  450.3 397.3 %all-reduce.15.cloned.1.call-done = (bf16[64,80,768]{2,1,0:T(8,128)(2,1)}, bf16[64,80,768]{2,1,0:T(8,128)(2,1)}, bf16[512,768]{1,0:T(8,128)(2,1)}) async-done(((bf16[64,80,768]{2,1,0:T(8,128)(2,1)}, bf16[64,80,768]{2,1,0:T(8,128)(2,1)}, bf16[512,768]{1,0:T(8,128)(2,1)}), (bf16[64,80,768]{2,1,0:T(8,128)(2,1)}, bf16[64,80,768]{2,1,0:T(8,128)(2,1)}, bf16[512,768]{1,0:T(8,128)(2,1)})) %all-reduce.15.cloned.1.call-update) | async-done | bytes 16515088 | tf_op jit(solution)/shard_map/psum | solution.py:72
  847.6 102.6 %all_to_all.20 = bf16[64,80,768]{2,1,0:T(8,128)(2,1)} all-to-all(bf16[64,80,768]{2,1,0:T(8,128)(2,1)} %get-tuple-element.33), channel_id=1, replica_groups=mesh['expert'=64,'tensor'=2] {'expert'}, dimensions={0} | all-to-all | bytes 15728640 | tf_op jit(solution)/shard_map/all_to_all | solution.py:73
  950.3 6.3 all-to-all-start.3
  962.6 8.2 multiply_reduce_fusion.1
  970.9 84.0 %all-to-all-done.3 = bf16[64,80,768]{2,1,0:T(8,128)(2,1)} async-done(((bf16[64,80,768]{2,1,0:T(8,128)(2,1)}), bf16[64,80,768]{2,1,0:T(8,128)(2,1)}, u32[]{:S(2)}, u32[]{:S(2)}) %all-to-all-start.3) | async-done | bytes 7864352 | tf_op jit(solution)/shard_map/all_to_all | solution.py:73
  1060.1 7.4 fusion.133
  1071.4 10.2 fusion.134
  1081.7 13.2 fusion.25
  1094.9 46.7 %fusion.8 = f32[6,64,2048]{2,1,0:T(8,128)} fusion(f32[6,512,2048]{2,1,0:T(8,128)} %fusion.134, f32[6,512,2048]{2,1,0:T(8,128)} %get-tuple-element.65, f32[6,512]{1,0:T(8,128)} %log_add_fusion, pred[512,2048]{1,0:T(8,128)(4,1)} %copy-done.9, bf16[512,6,32]{0,2,1:T(8,128)(2,1)S(1)} %copy-done.44, bf16[512,6,32]{0,2,1:T(8,128)(2,1)S(1)} %copy-done.43), kind=kOutput, calls=%fused_computation.14 | convolution fusion | flops 875303936 | bytes 54931456 | tf_op jit(solution)/shard_map/hqk,qhd->khd/dot_general | solution.py:297
  1156.2 45.5 %fusion.61 = f32[512,6,64]{0,2,1:T(8,128)} fusion(bf16[2048,6,64]{0,2,1:T(8,128)(2,1)} %bitcast.164, f32[6,512,2048]{2,1,0:T(8,128)} %fusion.134, f32[6,512,2048]{2,1,0:T(8,128)} %get-tuple-element.65, f32[6,512]{1,0:T(8,128)} %log_add_fusion, pred[512,2048]{1,0:T(8,128)(4,1)} %copy-done.9), kind=kOutput, calls=%fused_computation.94 | convolution fusion | flops 874517504 | bytes 53751808 | tf_op jit(solution)/shard_map/hqk,khd->qhd/dot_general | solution.py:294
  1223.1 7.3 convolution_bitcast_fusion
  1230.3 6.5 convolution_bitcast_fusion.1
  1236.8 6.9 convolution_bitcast_fusion.2
  1243.9 43.4 %all-reduce.13.cloned.1.call-done = (bf16[512,768]{1,0:T(8,128)(2,1)}, bf16[512,768]{1,0:T(8,128)(2,1)}) async-done(((bf16[512,768]{1,0:T(8,128)(2,1)}, bf16[512,768]{1,0:T(8,128)(2,1)}), (bf16[512,768]{1,0:T(8,128)(2,1)}, bf16[512,768]{1,0:T(8,128)(2,1)})) %all-reduce.13.cloned.1.call-update) | async-done | bytes 1572880 | tf_op jit(solution)/shard_map/psum | solution.py:60
  1289.2 322.4 %all-reduce = (f32[768]{0:T(1024)}, f32[768]{0:T(1024)}, f32[768,16]{0,1:T(8,128)}) all-reduce(f32[768]{0:T(1024)S(1)} %get-tuple-element.19, f32[768]{0:T(1024)S(1)} %copy-done.77, f32[768,16]{0,1:T(8,128)S(1)} %fusion.141), channel_id=1, replica_groups=mesh['expert'=64,'tensor'=2] {'expert'}, use_global_device_ids=true, to_apply=%region_27.28 | all-reduce | flops 13824 | bytes 110592 | tf_op jit(solution)/shard_map/psum | solution.py:338
  1615.7 357.3 %all-reduce.11.cloned.1.call-done = (f32[768,384]{1,0:T(8,128)}, f32[768,384]{1,0:T(8,128)}, f32[768,384]{1,0:T(8,128)}, f32[384,768]{1,0:T(8,128)}, f32[768,102...) async-done(((f32[768,384]{1,0:T(8,128)}, f32[768,384]{1,0:T(8,128)}, f32[768,384]{1,0:T(8,128)}, f32[384,768]{1,0:T(8,128)}, f32[768,1024]{1,0:T(8,128)}, ...) | async-done | bytes 14155792 | tf_op jit(solution)/shard_map/psum | solution.py:338
  (281 shorter events, 153.2 us)
Async XLA Ops:
  7.2 315.3 %copy-start = (bf16[768,1024]{1,0:T(8,128)(2,1)S(1)}, bf16[768,1024]{1,0:T(8,128)(2,1)}, u32[]{:S(2)}) copy-start(bf16[768,1024]{1,0:T(8,128)(2,1)} %param.26) | copy-start | bytes 4718596
  7.2 163.2 %all-reduce.9.cloned.1.call-start = ((), (), s32[]{:S(2)}) async-start(), calls=%async_computation.4 | async-start | bytes 1572864 | tf_op jit(solution)/shard_map/psum | solution.py:60
  15.3 14.6 copy-start.66
  16.6 13.6 copy-start.19
  17.6 19.7 collective-permute-start.2
  22.2 31.9 %collective-permute-start.1 = (bf16[2,512,384]{2,1,0:T(8,128)(2,1)}, bf16[2,512,384]{2,1,0:T(8,128)(2,1)}, u32[]{:S(2)}, u32[]{:S(2)}) collective-permute-start(bf16[2,512,384]{2,1,0:T(8,128)(2,1)} %pad_maximum_fusion.1), channel_id=1, source_target_pairs={{0,4},{2,6},{4,8},{6,10},{8,12},{10,14},{12,16},{14,18},{16,20},{1... | collective-permute-start | bytes 2359304 | tf_op jit(solution)/shard_map/ppermute | solution.py:20
  26.3 38.9 %collective-permute-start = (bf16[2,512,384]{2,1,0:T(8,128)(2,1)}, bf16[2,512,384]{2,1,0:T(8,128)(2,1)}, u32[]{:S(2)}, u32[]{:S(2)}) collective-permute-start(bf16[2,512,384]{2,1,0:T(8,128)(2,1)} %pad_maximum_fusion.1), channel_id=1, source_target_pairs={{0,6},{2,8},{4,10},{6,12},{8,14},{10,16},{12,18},{14,20},{16,22},{... | collective-permute-start | bytes 2359304 | tf_op jit(solution)/shard_map/ppermute | solution.py:20
  31.4 71.4 %copy-start.9 = (pred[512,2048]{1,0:T(8,128)(4,1)}, pred[512,2048]{1,0:T(8,128)(4,1)S(1)}, u32[]{:S(2)}) copy-start(pred[512,2048]{1,0:T(8,128)(4,1)S(1)} %compare_and_fusion) | copy-start | bytes 3145732
  90.8 12.1 copy-start.15
  102.8 11.9 copy-start.64
  102.9 12.6 copy-start.27
  121.7 50.4 %copy-start.71 = (f32[768]{0:T(1024)S(1)}, f32[768]{0:T(1024)}, u32[]{:S(2)}) copy-start(f32[768]{0:T(1024)} %param.23) | copy-start | bytes 9220
  122.5 69.3 %copy-start.78 = (s32[512,2]{0,1:T(2,128)}, s32[512,2]{0,1:T(2,128)S(1)}, u32[]{:S(2)}) copy-start(s32[512,2]{0,1:T(2,128)S(1)} %multiply_add_fusion.1) | copy-start | bytes 12292
  178.4 12.9 copy-start.59
  178.4 108.9 %all-to-all-start = ((bf16[64,80,768]{2,1,0:T(8,128)(2,1)}), bf16[64,80,768]{2,1,0:T(8,128)(2,1)}, u32[]{:S(2)}, u32[]{:S(2)}) async-start(bf16[64,80,768]{2,1,0:T(8,128)(2,1)} %bitcast.156), calls=%async_computation | async-start | bytes 15728640 | tf_op jit(solution)/shard_map/all_to_all | solution.py:65
  292.5 124.1 %all-to-all-start.2 = ((bf16[64,80,768]{2,1,0:T(8,128)(2,1)}), bf16[64,80,768]{2,1,0:T(8,128)(2,1)}, u32[]{:S(2)}, u32[]{:S(2)}) async-start(bf16[64,80,768]{2,1,0:T(8,128)(2,1)} %bitcast.155), calls=%async_computation.2 | async-start | bytes 15728640 | tf_op jit(solution)/shard_map/all_to_all | solution.py:65
  318.2 529.4 %all-reduce.15.cloned.1.call-start = ((), (), s32[]{:S(2)}) async-start(), calls=%async_computation.7 | async-start | bytes 33030144 | tf_op jit(solution)/shard_map/psum | solution.py:72
  336.0 80.6 %copy-start.52 = (bf16[1,256,768]{2,1,0:T(8,128)(2,1)S(1)}, bf16[1,256,768]{2,1,0:T(8,128)(2,1)}, u32[]{:S(2)}) copy-start(bf16[1,256,768]{2,1,0:T(8,128)(2,1)} %param.30) | copy-start | bytes 1179652
  426.4 13.1 copy-start.3
  950.3 104.6 %all-to-all-start.3 = ((bf16[64,80,768]{2,1,0:T(8,128)(2,1)}), bf16[64,80,768]{2,1,0:T(8,128)(2,1)}, u32[]{:S(2)}, u32[]{:S(2)}) async-start(bf16[64,80,768]{2,1,0:T(8,128)(2,1)} %get-tuple-element.34), calls=%async_computation.3 | async-start | bytes 15728640 | tf_op jit(solution)/shard_map/all_to_all | solution.py:73
  956.6 330.8 %all-reduce.13.cloned.1.call-start = ((), (), s32[]{:S(2)}) async-start(), calls=%async_computation.6 | async-start | bytes 3145728 | tf_op jit(solution)/shard_map/psum | solution.py:60
  1071.4 10.3 copy-start.10
  1071.4 10.3 copy-start.80
  1081.7 13.2 copy-start.43
  1081.7 13.2 copy-start.44
  1146.6 55.2 %collective-permute-start.3 = (bf16[2,512,384]{1,2,0:T(8,128)(2,1)}, bf16[2,512,384]{1,2,0:T(8,128)(2,1)}, u32[]{:S(2)}, u32[]{:S(2)}) collective-permute-start(bf16[2,512,384]{1,2,0:T(8,128)(2,1)} %get-tuple-element.42), channel_id=1, source_target_pairs={{2,0},{4,2},{6,4},{8,6},{10,8},{12,10},{14,12},{16,14},{18,16},{20... | collective-permute-start | bytes 2359304 | tf_op jit(solution)/shard_map/ppermute | solution.py:20
  1149.0 52.7 %collective-permute-start.5 = (bf16[2,512,384]{1,2,0:T(8,128)(2,1)}, bf16[2,512,384]{1,2,0:T(8,128)(2,1)}, u32[]{:S(2)}, u32[]{:S(2)}) collective-permute-start(bf16[2,512,384]{1,2,0:T(8,128)(2,1)} %get-tuple-element.43), channel_id=1, source_target_pairs={{6,0},{8,2},{10,4},{12,6},{14,8},{16,10},{18,12},{20,14},{22,16},{... | collective-permute-start | bytes 2359304 | tf_op jit(solution)/shard_map/ppermute | solution.py:20
  1150.3 51.4 %collective-permute-start.4 = (bf16[2,512,384]{1,2,0:T(8,128)(2,1)}, bf16[2,512,384]{1,2,0:T(8,128)(2,1)}, u32[]{:S(2)}, u32[]{:S(2)}) collective-permute-start(bf16[2,512,384]{1,2,0:T(8,128)(2,1)} %get-tuple-element.44), channel_id=1, source_target_pairs={{4,0},{6,2},{8,4},{10,6},{12,8},{14,10},{16,12},{18,14},{20,16},{2... | collective-permute-start | bytes 2359304 | tf_op jit(solution)/shard_map/ppermute | solution.py:20
  1209.4 763.6 %all-reduce.11.cloned.1.call-start = ((), (), s32[]{:S(2)}) async-start(), calls=%async_computation.5 | async-start | bytes 28311552 | tf_op jit(solution)/shard_map/psum | solution.py:338
  1236.8 50.5 %copy-start.58 = (f32[768]{0:T(1024)S(1)}, f32[768]{0:T(1024)}, u32[]{:S(2)}) copy-start(f32[768]{0:T(1024)} %param.18) | copy-start | bytes 9220
  1236.8 50.5 %copy-start.63 = (f32[512]{0:T(512)S(1)}, f32[512]{0:T(512)}, u32[]{:S(2)}) copy-start(f32[512]{0:T(512)} %copy-done.61) | copy-start | bytes 6148
  1236.8 52.3 %copy-start.77 = (f32[768]{0:T(1024)S(1)}, f32[768]{0:T(1024)}, u32[]{:S(2)}) copy-start(f32[768]{0:T(1024)} %get-tuple-element.15) | copy-start | bytes 9220
  (66 other events, 277.0 us)
Sparse Core Ops, SparseCore 0:
  117.1 53.3 all-reduce.8
  450.5 397.1 all-reduce.14
  1209.5 77.7 all-reduce.12
  1291.7 681.2 all-reduce.10
where the time goes:
time: 2000 us; the launch traced here: 1990 us
  waiting for transfers between devices  1120 us (56%)
  blocking collectives  425 us (21%)
  matrix products  273 us (14%)
  starting transfers between devices  60.6 us (3%)
  other arithmetic  58.1 us (3%)
  local copies, waits for them, and re-layouts  37.6 us (2%)
    psum x1, waiting for transfers between devices, from_owner(): summed = lax.psum(shaped.astype(jnp.bfloat16), 'tensor')  397 us
    psum x1, waiting for transfers between devices, local(): lax.psum((grad_w_query, grad_w_key, grad_w_value, grad_w_output, grad_gai...  357 us
    psum x1, blocking collectives, local(): lax.psum((grad_w_query, grad_w_key, grad_w_value, grad_w_output, grad_gai...  322 us
    all_to_all x2, waiting for transfers between devices, to_owner(): lax.all_to_all(copies, 'expert', split_axis=0, concat_axis=0, tiled=True)  163 us
    all_to_all x1, blocking collectives, from_owner(): lax.all_to_all(summed, 'expert', split_axis=0, concat_axis=0, tiled=True)  103 us
    psum x2, waiting for transfers between devices, tensor_sum(): return lax.psum(values.astype(jnp.bfloat16), 'tensor').astype(jnp.float32)  88.6 us
    all_to_all x1, waiting for transfers between devices, from_owner(): lax.all_to_all(summed, 'expert', split_axis=0, concat_axis=0, tiled=True)  84 us
    dot_general x1, matrix products, local(): jnp.einsum('hqk,qhd->khd', score_grads, query_rot, preferred_element_type...  46.7 us
  transfers between devices with their start and end apart: 13, of which 10 were waited for; matrix products, arithmetic and copies ran while one was open for 7% of the time, Pallas kernels for 0%

commit v1 on v0

v1 whole, which is shorter than its diff:
```python
import jax
import jax.numpy as jnp
import numpy as np
from jax import lax
from jax.sharding import Mesh
from jax.sharding import PartitionSpec as P

HEAD_DIM = 64
BLOCK = 256
SLOTS = 40
AXES = ("zh", "x", "yh", "yl", "c", "t")
EXPERT = AXES[:5]
ROUTE = ("zh", "x", "yh")
PLANE = ("x", "yh", "yl")

epsilon = 1e-06
rope_base = 10000.0
masked_out = -1e30
bf16 = jnp.bfloat16
f32 = jnp.float32


def swap(x, axis):
    return lax.ppermute(x, axis, [(0, 1), (1, 0)])


def exchange(x, axis):
    return lax.all_to_all(x, axis, split_axis=0, concat_axis=0, tiled=True)


def dot(a, b, dims=((1,), (0,))):
    return lax.dot_general(a, b, (dims, ((), ())), preferred_element_type=f32)


def dot_nt(a, b):
    return dot(a, b, ((1,), (1,)))


def dot_tn(a, b):
    return dot(a, b, ((0,), (0,)))


def swish_unit(values):
    return values * jax.nn.sigmoid(values)


def swish_slope(values):
    sigmoid = jax.nn.sigmoid(values)
    return sigmoid * (1.0 + values * (1.0 - sigmoid))


def rms_scale(values):
    return lax.rsqrt(jnp.mean(values * values, axis=-1, keepdims=True) + epsilon)


def pair_sum(values, axis):
    low = values.astype(bf16)
    return low.astype(f32) + swap(low, axis).astype(f32)


def norm_back(inputs, row_scale, gain_row, upstream):
    unit_rows = inputs * row_scale
    scaled_grad = upstream * gain_row
    return row_scale * (
        scaled_grad - unit_rows * jnp.mean(scaled_grad * unit_rows, axis=-1, keepdims=True)
    )


def half_by(values, bit):
    rows = values.shape[0] // 2
    first, second = values[:rows], values[rows:]
    return jnp.where(bit == 0, first, second), jnp.where(bit == 0, second, first)


def sum_over_expert(values, core):
    rows, width = values.shape
    kept, given = half_by(values, core)
    kept = kept + swap(given.astype(bf16), "c").astype(f32)
    parts = exchange(kept.astype(bf16).reshape(16, rows // 32, width), PLANE)
    part = jnp.sum(parts.astype(f32), axis=0)
    part = pair_sum(part, "zh").astype(bf16)
    copies = jnp.broadcast_to(part[None], (16, rows // 32, width))
    mine = exchange(copies, PLANE).reshape(rows // 2, width)
    theirs = swap(mine, "c")
    return jnp.concatenate(
        [jnp.where(core == 0, mine, theirs), jnp.where(core == 0, theirs, mine)], axis=0
    ).astype(f32)


def local(
    tokens,
    routes,
    gain_one,
    w_query,
    w_key,
    w_value,
    w_output,
    gain_two,
    w_router,
    shared_gate,
    shared_up,
    shared_down,
    expert_gate,
    expert_up,
    expert_down,
    cotangent,
):
    rows, width = tokens.shape
    wide = w_query.shape[1]
    heads_here = wide // HEAD_DIM
    experts = w_router.shape[1]
    seats = experts * SLOTS
    tensor = lax.axis_index("t")
    core = lax.axis_index("c")
    high = lax.axis_index("yl")
    expert_here = lax.axis_index(ROUTE)
    score_scale = HEAD_DIM ** (-0.5)
    place_of = [
        (high ^ my) * 2 + (core ^ mc) for my, mc in ((0, 0), (0, 1), (1, 0), (1, 1))
    ]
    own_place = place_of[0]

    tokens_y = swap(tokens, "yl")
    tokens_c = swap(tokens, "c")
    tokens_yc = swap(tokens_y, "c")
    all_tokens = jnp.concatenate([tokens, tokens_c, tokens_y, tokens_yc], axis=0)

    own_weights = jnp.concatenate([expert_gate[0], expert_up[0], expert_down[0].T], axis=1)[None]
    weights = jnp.concatenate([own_weights, swap(own_weights, "t")], axis=0)
    weights = jnp.concatenate([weights, swap(weights, "yl")], axis=0)
    weights = jnp.concatenate([weights, swap(weights, "c")], axis=0)

    flat_routes = routes.reshape(-1)
    expert_ids = jnp.arange(experts, dtype=jnp.int32)
    matches = (flat_routes[:, None] == expert_ids[None, :]).astype(jnp.int32)
    before = jnp.cumsum(matches, axis=0) - matches
    slot_index = jnp.sum(before * matches, axis=-1) - tensor * SLOTS
    seat = jnp.where(
        (slot_index >= 0) & (slot_index < SLOTS), flat_routes * SLOTS + slot_index, -1
    ).reshape(rows, -1)
    seat_ids = jnp.arange(seats, dtype=jnp.int32)
    placer = jnp.sum((seat[:, :, None] == seat_ids[None, None, :]).astype(f32), axis=1).astype(bf16)
    extra = jnp.where(
        jnp.arange(128)[None, :] == 0, jnp.sum(routes, axis=1, keepdims=True).astype(f32), 0.0
    ).astype(bf16)
    sent_cot = dot_tn(placer, jnp.concatenate([cotangent, extra], axis=1)).astype(bf16)
    cot_ext = exchange(sent_cot.reshape(experts, SLOTS, -1), ROUTE).reshape(seats, -1)
    cot_rows = cot_ext[:, :width]
    other_expert = cot_ext[:, width : width + 1].astype(jnp.int32) - expert_here

    all_stream = all_tokens.astype(f32)
    all_unit = all_stream * rms_scale(all_stream)
    all_normed = (all_unit * gain_one).astype(bf16)
    stream = tokens.astype(f32)
    scale_one = rms_scale(stream)
    normed = all_normed[:rows]
    frequency = rope_base ** (-np.arange(HEAD_DIM // 2) * 2.0 / HEAD_DIM)
    key_places = jnp.concatenate(
        [place * rows + jnp.arange(rows, dtype=jnp.int32) for place in place_of]
    )
    angles = key_places.astype(f32)[:, None] * frequency.astype(np.float32)[None, :]
    cosine, sine = jnp.cos(angles)[:, None, :], jnp.sin(angles)[:, None, :]

    def rotary(values, direction):
        count = values.shape[0]
        cos, sin = cosine[:count], direction * sine[:count]
        leading, trailing = values[..., : HEAD_DIM // 2], values[..., HEAD_DIM // 2 :]
        return jnp.concatenate(
            [leading * cos - trailing * sin, trailing * cos + leading * sin], axis=-1
        )

    query_rot = rotary(dot(normed, w_query).reshape(rows, heads_here, HEAD_DIM), 1.0).astype(bf16)
    all_keys = rotary(dot(all_normed, w_key).reshape(4 * rows, heads_here, HEAD_DIM), 1.0).astype(
        bf16
    )
    all_values = dot(all_normed, w_value).astype(bf16).reshape(4 * rows, heads_here, HEAD_DIM)
    query_places = key_places[:rows]
    allowed = key_places[None, :] // BLOCK <= query_places[:, None] // BLOCK

    def scores_of():
        raw = jnp.einsum("qhd,khd->hqk", query_rot, all_keys, preferred_element_type=f32)
        return jnp.where(allowed[None], raw * score_scale, masked_out)

    scores = scores_of()
    highest = jnp.max(scores, axis=-1, keepdims=True)
    weigh = jnp.exp(scores - highest)
    weight_sum = jnp.sum(weigh, axis=-1, keepdims=True)
    attention = weigh / weight_sum
    log_total = highest + jnp.log(weight_sum)
    mixed_heads = (
        jnp.einsum("hqk,khd->qhd", attention.astype(bf16), all_values, preferred_element_type=f32)
        .astype(bf16)
        .reshape(rows, -1)
    )
    middle = stream + pair_sum(dot(mixed_heads, w_output), "t")
    scale_two = rms_scale(middle)
    unit_two = middle * scale_two
    normed_two = (unit_two * gain_two).astype(bf16)

    sent_rows = dot_tn(placer, normed_two).astype(bf16)
    rows_in = exchange(sent_rows.reshape(experts, SLOTS, width), ROUTE).reshape(seats, width)
    row_logits = dot(rows_in, w_router)
    own_logit = jnp.sum(jnp.where(expert_ids[None, :] == expert_here, row_logits, 0.0), axis=1, keepdims=True)
    other_logit = jnp.sum(jnp.where(expert_ids[None, :] == other_expert, row_logits, 0.0), axis=1, keepdims=True)
    top_logit = jnp.maximum(own_logit, other_logit)
    own_weight = jnp.exp(own_logit - top_logit)
    row_share = own_weight / (own_weight + jnp.exp(other_logit - top_logit))
    part = wide_part = expert_gate.shape[2]
    gates, ups = weights[:, :, :part], weights[:, :, part : 2 * part]
    downs = weights[:, :, 2 * part :]
    gate_expert = jnp.einsum("rd,kdf->krf", rows_in, gates, preferred_element_type=f32)
    up_expert = jnp.einsum("rd,kdf->krf", rows_in, ups, preferred_element_type=f32)
    hidden_grads = jnp.einsum("rd,kdf->krf", cot_rows, downs, preferred_element_type=f32)
    hidden_expert = (swish_unit(gate_expert) * up_expert).astype(bf16)
    gate_dots = jnp.sum(hidden_expert.astype(f32) * hidden_grads, axis=(0, 2))[:, None]
    expert_gate_grads = (hidden_grads * up_expert * swish_slope(gate_expert)).astype(bf16)
    expert_up_grads = (hidden_grads * swish_unit(gate_expert)).astype(bf16)
    rows_part = jnp.einsum("krf,kdf->rd", expert_gate_grads, gates, preferred_element_type=f32)
    rows_part = rows_part + jnp.einsum(
        "krf,kdf->rd", expert_up_grads, ups, preferred_element_type=f32
    )
    dots_high = gate_dots.astype(bf16).astype(f32)
    lanes = jnp.arange(128)[None, :]
    dots_ext = jnp.where(lanes == expert_here, dots_high, 0.0) + jnp.where(
        lanes == experts + expert_here, gate_dots - dots_high, 0.0
    )
    back = jnp.concatenate([row_share * rows_part, dots_ext], axis=1).astype(bf16)
    back = exchange(back.reshape(experts, SLOTS, -1), ROUTE).reshape(seats, -1)
    expert_out = jnp.einsum("krf,kdf->rd", hidden_expert, downs, preferred_element_type=f32)
    picked = exchange(
        (row_share * expert_out).astype(bf16).reshape(experts, SLOTS, width), ROUTE
    ).reshape(seats, width)

    scaled_rows = (row_share * rows_in.astype(f32)).astype(bf16)
    out_grads = (row_share * cot_rows.astype(f32)).astype(bf16)
    grad_gates = jnp.einsum("rd,krf->kdf", scaled_rows, expert_gate_grads, preferred_element_type=f32)
    grad_ups = jnp.einsum("rd,krf->kdf", scaled_rows, expert_up_grads, preferred_element_type=f32)
    grad_downs = jnp.einsum("rd,krf->kdf", out_grads, hidden_expert, preferred_element_type=f32)
    grads = jnp.concatenate([grad_gates, grad_ups, grad_downs], axis=2).astype(bf16)
    grads = grads[:4].astype(f32) + swap(grads[4:], "c").astype(f32)
    grads = grads.astype(bf16)
    grads = grads[:2].astype(f32) + swap(grads[2:], "yl").astype(f32)
    grads = grads.astype(bf16)
    grads = grads[0].astype(f32) + swap(grads[1], "t").astype(f32)
    grad_expert_gate = grads[None, :, :part]
    grad_expert_up = grads[None, :, part : 2 * part]
    grad_expert_down = grads[:, 2 * part :].T[None]

    gate_shared = dot(normed_two, shared_gate)
    up_shared = dot(normed_two, shared_up)
    hidden_shared = (swish_unit(gate_shared) * up_shared).astype(bf16)
    shared_hidden_grads = dot_nt(cotangent, shared_down)
    shared_gate_grads = (shared_hidden_grads * up_shared * swish_slope(gate_shared)).astype(bf16)
    shared_up_grads = (shared_hidden_grads * swish_unit(gate_shared)).astype(bf16)
    shared_back = dot_nt(shared_gate_grads, shared_gate) + dot_nt(shared_up_grads, shared_up)
    shared_out = dot(hidden_shared, shared_down)
    grad_shared_down = dot_tn(hidden_shared, cotangent)
    grad_shared_gu = dot_tn(normed_two, jnp.concatenate([shared_gate_grads, shared_up_grads], axis=1))

    logits = dot(normed_two, w_router)
    choose = routes[:, :, None] == expert_ids[None, None, :]
    chosen = jnp.sum(jnp.where(choose, logits[:, None, :], 0.0), axis=-1)
    gate_weights = jnp.exp(chosen - jnp.max(chosen, axis=1, keepdims=True))
    gate_share = gate_weights / jnp.sum(gate_weights, axis=1, keepdims=True)
    share = jnp.sum(jnp.where(choose, gate_share[:, :, None], 0.0), axis=1)
    combined = dot(placer, back)
    routed_grads = combined[:, :width]
    gate_grads = combined[:, width : width + experts] + combined[:, width + experts : width + 2 * experts]
    logits_grads = (
        share * (gate_grads - jnp.sum(share * gate_grads, axis=1, keepdims=True))
    ).astype(bf16)
    grad_router = dot_tn(normed_two, logits_grads)
    router_back = dot_nt(logits_grads, w_router)
    normed_two_grads = pair_sum(shared_back + router_back + routed_grads, "t")
    grad_gain_two = jnp.sum(normed_two_grads * unit_two, axis=0)
    grad_result = cotangent.astype(f32)
    middle_grads = grad_result + norm_back(middle, scale_two, gain_two, normed_two_grads)
    middle_low = middle_grads.astype(bf16)
    block_out = (middle + pair_sum(shared_out + dot(placer, picked), "t")).astype(bf16)

    mixed_grads = dot_nt(middle_low, w_output).astype(bf16).reshape(rows, heads_here, HEAD_DIM)
    attention = jnp.exp(scores_of() - log_total)
    prob_grads = jnp.einsum("qhd,khd->hqk", mixed_grads, all_values, preferred_element_type=f32)
    value_full = jnp.einsum("hqk,qhd->khd", attention.astype(bf16), mixed_grads, preferred_element_type=f32)
    score_grads = (
        attention
        * (prob_grads - jnp.sum(prob_grads * attention, axis=-1, keepdims=True))
        * score_scale
    ).astype(bf16)
    query_full = jnp.einsum("hqk,khd->qhd", score_grads, all_keys, preferred_element_type=f32)
    key_full = jnp.einsum("hqk,qhd->khd", score_grads, query_rot, preferred_element_type=f32)
    query_grads = rotary(query_full, -1.0).reshape(rows, -1).astype(bf16)
    key_grads = rotary(key_full, -1.0).reshape(4 * rows, -1).astype(bf16)
    value_grads = value_full.reshape(4 * rows, -1).astype(bf16)
    normed_part = dot_nt(key_grads, w_key) + dot_nt(value_grads, w_value)
    own_part = normed_part[:rows] + dot_nt(query_grads, w_query)
    y_part = normed_part[2 * rows : 3 * rows]
    given = jnp.stack([normed_part[rows : 2 * rows], normed_part[3 * rows :]]).astype(bf16)
    taken = swap(given, "c").astype(f32)
    own_part = own_part + taken[0]
    own_part = own_part + swap((y_part + taken[1]).astype(bf16), "yl").astype(f32)
    normed_grads = pair_sum(own_part, "t")
    grad_tokens = middle_grads + norm_back(stream, scale_one, gain_one, normed_grads)

    grad_query = dot_tn(normed, query_grads)
    grad_key = dot_tn(all_normed, key_grads)
    grad_value = dot_tn(all_normed, value_grads)
    gain_part = (
        jnp.sum(
            grad_query * w_query.astype(f32)
            + grad_key * w_key.astype(f32)
            + grad_value * w_value.astype(f32),
            axis=1,
        )
        / gain_one
    )
    grad_output = dot_tn(middle_low, mixed_heads)
    small = jnp.concatenate(
        [
            grad_router,
            gain_part[:, None],
            grad_gain_two[:, None],
            jnp.zeros((width, 128 - experts - 2), f32),
        ],
        axis=1,
    )
    shared_gu = sum_over_expert(grad_shared_gu, core)
    grad_shared_down = sum_over_expert(grad_shared_down, core)
    packed = sum_over_expert(
        jnp.concatenate([grad_query, grad_key, grad_value, grad_output, small], axis=1), core
    )
    small = packed[:, 4 * wide :]
    both = small + swap(small, "t")
    return (
        block_out,
        grad_tokens,
        both[:, experts],
        packed[:, :wide],
        packed[:, wide : 2 * wide],
        packed[:, 2 * wide : 3 * wide],
        packed[:, 3 * wide : 4 * wide].T,
        small[:, experts + 1],
        both[:, :experts],
        shared_gu[:, : shared_gate.shape[1]],
        shared_gu[:, shared_gate.shape[1] :],
        grad_shared_down,
        grad_expert_gate,
        grad_expert_up,
        grad_expert_down,
    )


def solution(mesh):
    fine = Mesh(mesh.devices.reshape(2, 4, 2, 2, 2, 2), AXES)
    placed = (
        P(EXPERT, None),
        P(EXPERT, None),
        P(),
        P(None, "t"),
        P(None, "t"),
        P(None, "t"),
        P("t", None),
        P(),
        P(),
        P(None, "t"),
        P(None, "t"),
        P("t", None),
        P(EXPERT, None, "t"),
        P(EXPERT, None, "t"),
        P(EXPERT, "t", None),
        P(EXPERT, None),
    )
    return jax.shard_map(
        local,
        mesh=fine,
        in_specs=placed,
        out_specs=(
            P(EXPERT, None),
            P(EXPERT, None),
            P(),
            P(None, "t"),
            P(None, "t"),
            P(None, "t"),
            P("t", None),
            P(),
            P(),
            P(None, "t"),
            P(None, "t"),
            P("t", None),
            P(EXPERT, None, "t"),
            P(EXPERT, None, "t"),
            P(EXPERT, "t", None),
        ),
        check_vma=False,
    )
```

time: 2000 us -> 695 us (0.35)
  waiting for transfers between devices: 1120 us -> 170 us
  blocking collectives: 425 us -> 0 us
  other arithmetic: 58.1 us -> 116 us
  matrix products: 273 us -> 217 us
  local copies, waits for them, and re-layouts: 37.6 us -> 80.8 us
  starting transfers between devices: 60.6 us -> 102 us
    psum x4 -> x0, waiting for transfers between devices: 843 us -> none  [the longest x1 397 us: from_owner(): summed = lax.psum(shaped.astype(jnp.bfloat16), 'tensor')]
    psum x1 -> x0, blocking collectives: 322 us -> none  [local(): lax.psum((grad_w_query, grad_w_key, grad_w_value, grad_w_output, grad_gai...]
    all_to_all x3 -> x10, waiting for transfers between devices: 247 us -> 80.7 us  [exchange(): return lax.all_to_all(x, axis, split_axis=0, concat_axis=0, tiled=True)]
    all_to_all x1 -> x0, blocking collectives: 103 us -> none  [from_owner(): lax.all_to_all(summed, 'expert', split_axis=0, concat_axis=0, tiled=True)]
    ppermute x6 -> x25, waiting for transfers between devices: 33.7 us -> 88.9 us  [swap(): return lax.ppermute(x, axis, [(0, 1), (1, 0)])]
    dot_general x40, matrix products: 171 us -> 134 us  [the longest x28 51.2 us: dot(): return lax.dot_general(a, b, (dims, ((), ())), preferred_element_type=f32)]
    convert_element_type x3 -> x24, other arithmetic: 3.83 us -> 37.7 us  [the longest x3 8.05 us: sum_over_expert(): parts = exchange(kept.astype(bf16).reshape(16, rows // 32, width), PLANE)]
    ppermute x6 -> x25, starting transfers between devices: 17.3 us -> 38.6 us  [swap(): return lax.ppermute(x, axis, [(0, 1), (1, 0)])]
  transfers between devices with their start and end apart: 13 -> 35, of which waited for: 10 -> 13; matrix products, arithmetic and copies ran while one was open for 7% -> 58% of each run, Pallas kernels for 0% -> 0%
where the time goes in v1:
time: 695 us; the launch traced here: 688 us
  matrix products  217 us (31%)
  waiting for transfers between devices  170 us (24%)
  other arithmetic  116 us (17%)
  starting transfers between devices  102 us (15%)
  local copies, waits for them, and re-layouts  80.8 us (12%)
    ppermute x25, waiting for transfers between devices, swap(): return lax.ppermute(x, axis, [(0, 1), (1, 0)])  88.9 us
    all_to_all x10, waiting for transfers between devices, exchange(): return lax.all_to_all(x, axis, split_axis=0, concat_axis=0, tiled=True)  80.7 us
    all_to_all x10, starting transfers between devices, exchange(): return lax.all_to_all(x, axis, split_axis=0, concat_axis=0, tiled=True)  63 us
    dot_general x28, matrix products, dot(): return lax.dot_general(a, b, (dims, ((), ())), preferred_element_type=f32)  51.2 us
    ppermute x25, starting transfers between devices, swap(): return lax.ppermute(x, axis, [(0, 1), (1, 0)])  38.6 us
    dot_general x1, matrix products, local(): jnp.einsum('hqk,qhd->khd', score_grads, query_rot, preferred_element_type...  36.7 us
    dot_general x1, matrix products, local(): jnp.einsum('hqk,khd->qhd', score_grads, all_keys, preferred_element_type=...  36.1 us
    unnamed x207, local copies, waits for them, and re-layouts  32.6 us
  transfers between devices with their start and end apart: 35, of which 13 were waited for; matrix products, arithmetic and copies ran while one was open for 58% of the time, Pallas kernels for 0%

profile of v1, /device:TPU:1, one launch (start us, length us, event | category | flops | bytes accessed | tf_op | source)
XLA Modules:
  0.0 688.0 jit_solution(8891320794732965802)
XLA Ops:
  11.9 9.3 %reduce-window.6 = s32[16,8,128]{2,1,0:T(8,128)} reduce-window(s32[16,8,128]{2,1,0:T(8,128)} %fusion.117, s32[]{:T(128)} %constant.83.clone.1), window={size=1x1x128 pad=0_0x0_0x127_0}, to_apply=%region_4.5 | reduce-window | flops 2080768 | bytes 131076 | tf_op jit(solution)/shard_map/reduce-window
  52.9 10.6 %fusion.3 = (f32[6,512]{1,0:T(8,128)S(1)}, f32[6,512,2048]{2,1,0:T(8,128)}) fusion(pred[512,2048]{1,0:T(8,128)(4,1)S(1)} %broadcast_compare_fusion, bf16[2048,6,32]{0,2,1:T(8,128)(2,1)S(1)} %get-tuple-element.82, bf16[2048,6,32]{0,2,1:T(8,128)(2,1)S(1)} %get-tuple-element.81, bf16[512,6,32]{0,2,1:T(8,128)(2,1)S(1)} %get-tuple-element.99, ...), kind=kOutput, calls=%fused_computation.9 | convolution fusion | flops 828109824 | bytes 28192768 | tf_op jit(solution)/shard_map/qhd,khd->hqk/dot_general | solution.py:181
  63.5 12.0 %fusion.2 = f32[6,512]{1,0:T(8,128)S(1)} fusion(f32[6,512,2048]{2,1,0:T(8,128)} %get-tuple-element.113, f32[6,512]{1,0:T(8,128)S(1)} %get-tuple-element.112, pred[512,2048]{1,0:T(8,128)(4,1)S(1)} %broadcast_compare_fusion), kind=kLoop, calls=%fused_computation.8 | loop fusion | flops 25162752 | bytes 26238976 | tf_op jit(solution)/shard_map/reduce_sum | solution.py:187
  76.1 11.8 %fusion.93 = bf16[6,64,512]{2,1,0:T(8,128)(2,1)S(1)} fusion(bf16[2048,6,64]{0,2,1:T(8,128)(2,1)S(1)} %bitcast.245, f32[6,512,2048]{2,1,0:T(8,128)} %get-tuple-element.113, f32[6,512]{1,0:T(8,128)S(1)} %fusion.2, f32[6,512]{1,0:T(8,128)S(1)} %get-tuple-element.112, pred[512,2048]{1,0:T(8,128)(4,1)S(1)} %broadcast_compare_fusion), kind=kOutput, calls=%fused_computation.147 | convolution fusion | flops 836960256 | bytes 28205056 | tf_op jit(solution)/shard_map/hqk,khd->qhd/dot_general | solution.py:191
  91.6 9.6 %all-to-all-start.1 = ((bf16[16,40,896]{2,1,0:T(8,128)(2,1)}), bf16[16,40,896]{2,1,0:T(8,128)(2,1)}, u32[]{:S(2)}, u32[]{:S(2)}) async-start(bf16[16,40,896]{2,1,0:T(8,128)(2,1)} %bitcast.253), calls=%async_computation.1 | async-start | bytes 2293760 | tf_op jit(solution)/shard_map/all_to_all | solution.py:28
  106.7 12.7 %collective-permute-done.3 = bf16[512,768]{1,0:T(8,128)(2,1)} collective-permute-done((bf16[512,768]{1,0:T(8,128)(2,1)}, bf16[512,768]{1,0:T(8,128)(2,1)}, u32[]{:S(2)}, u32[]{:S(2)}) %collective-permute-start.3) | collective-permute-done | bytes 786464 | tf_op jit(solution)/shard_map/ppermute | solution.py:24
  135.7 9.5 %all-to-all-start = ((bf16[16,40,768]{2,1,0:T(8,128)(2,1)}), bf16[16,40,768]{2,1,0:T(8,128)(2,1)}, u32[]{:S(2)}, u32[]{:S(2)}) async-start(bf16[16,40,768]{2,1,0:T(8,128)(2,1)} %bitcast.255), calls=%async_computation | async-start | bytes 1966080 | tf_op jit(solution)/shard_map/all_to_all | solution.py:28
  145.2 31.0 %collective-permute-done.5 = bf16[2,768,768]{1,2,0:T(8,128)(2,1)} collective-permute-done((bf16[2,768,768]{1,2,0:T(8,128)(2,1)}, bf16[2,768,768]{1,2,0:T(8,128)(2,1)}, u32[]{:S(2)}, u32[]{:S(2)}) %collective-permute-start.5) | collective-permute-done | bytes 2359328 | tf_op jit(solution)/shard_map/ppermute | solution.py:24
  183.4 5.5 all-to-all-start.8
  195.3 5.3 add_convert_fusion.2
  202.4 5.0 all-to-all-start.6
  220.1 7.9 %all-to-all-done.6 = bf16[16,24,2048]{2,1,0:T(8,128)(2,1)} async-done(((bf16[16,24,2048]{2,1,0:T(8,128)(2,1)}), bf16[16,24,2048]{2,1,0:T(8,128)(2,1)}, u32[]{:S(2)}, u32[]{:S(2)}) %all-to-all-start.6) | async-done | bytes 1572896 | tf_op jit(solution)/shard_map/all_to_all | solution.py:28
  253.6 5.1 collective-permute-start.21
  267.3 6.7 collective-permute-start.18
  274.0 5.0 pad_maximum_fusion
  287.5 7.2 %fusion.39 = (f32[640]{0:T(1024)S(1)}, bf16[8,640,256]{1,2,0:T(8,128)(2,1)S(1)}, bf16[8,640,256]{1,2,0:T(8,128)(2,1)}, bf16[8,640,256]{1,2,0:T(8,128)(2,1)}) fusion(f32[8,256,640]{2,1,0:T(8,128)S(1)} %fusion.58, f32[8,256,640]{2,1,0:T(8,128)S(1)} %fusion.62, bf16[640,896]{1,0:T(8,128)(2,1)} %bitcast.10, bf16[8,768,768]{1,2,0:T(8,128)(2,1)S(1)} %pad_maximum_fusion), kind=kOutput, calls=%fused_computation.38 | convolution fusion | flops 2036858240 | bytes 22481408 | tf_op jit(solution)/shard_map/rd,kdf->krf/dot_general | solution.py:213
  297.8 6.0 all-to-all-start.2
  303.9 6.2 fusion.60
  310.2 5.7 fusion.70
  317.2 5.4 convert_bitcast_fusion.1
  322.6 9.2 %all-to-all-start.3 = ((bf16[16,40,896]{2,1,0:T(8,128)(2,1)}), bf16[16,40,896]{2,1,0:T(8,128)(2,1)}, u32[]{:S(2)}, u32[]{:S(2)}) async-start(bf16[16,40,896]{2,1,0:T(8,128)(2,1)} %pad_maximum_fusion.8), calls=%async_computation.3 | async-start | bytes 2293760 | tf_op jit(solution)/shard_map/all_to_all | solution.py:28
  331.8 6.5 convert_bitcast_fusion.2
  338.4 5.6 convert_bitcast_fusion
  364.7 18.2 %collective-permute-done.8 = bf16[512,768]{1,0:T(8,128)(2,1)S(1)} collective-permute-done((bf16[512,768]{1,0:T(8,128)(2,1)S(1)}, bf16[512,768]{1,0:T(8,128)(2,1)S(1)}, u32[]{:S(2)}, u32[]{:S(2)}) %collective-permute-start.8) | collective-permute-done | bytes 786464 | tf_op jit(solution)/shard_map/ppermute | solution.py:24
  387.8 10.6 %fusion.160 = f32[6,512,2048]{2,1,0:T(8,128)} fusion(bf16[512,6,64]{0,2,1:T(8,128)(2,1)S(1)} %bitcast.247, bf16[2048,6,64]{0,2,1:T(8,128)(2,1)S(1)} %bitcast.246), kind=kOutput, calls=%fused_computation.284 | convolution fusion | flops 805306368 | bytes 27131904 | tf_op jit(solution)/shard_map/qhd,khd->hqk/dot_general | solution.py:283
  398.4 36.1 %fusion.90 = f32[512,6,64]{0,2,1:T(8,128)} fusion(f32[6,512,2048]{2,1,0:T(8,128)} %fusion.160, f32[6,512,2048]{2,1,0:T(8,128)} %get-tuple-element.113, f32[6,512]{1,0:T(8,128)S(1)} %log_add_fusion, pred[512,2048]{1,0:T(8,128)(4,1)S(1)} %copy-done.34, bf16[2048,6,32]{0,2,1:T(8,128)(2,1)} %copy-done.71, bf16[2048,6,32]{0,2,1:T(8,128)(2,1)} %copy-done.70), kind=kOutput, calls=%fused_computation.143 | convolution fusion | flops 877663232 | bytes 53751808 | tf_op jit(solution)/shard_map/hqk,khd->qhd/dot_general | solution.py:290
  434.5 36.7 %fusion.46 = f32[2048,6,64]{0,2,1:T(8,128)} fusion(f32[6,512,2048]{2,1,0:T(8,128)} %fusion.160, f32[6,512,2048]{2,1,0:T(8,128)} %get-tuple-element.113, f32[6,512]{1,0:T(8,128)S(1)} %log_add_fusion, pred[512,2048]{1,0:T(8,128)(4,1)S(1)} %copy-done.34, bf16[512,6,32]{0,2,1:T(8,128)(2,1)S(1)} %copy-done.80, bf16[512,6,32]{0,2,1:T(8,128)(2,1)S(1)} %copy-done.78), kind=kOutput, calls=%fused_computation.59 | convolution fusion | flops 875303936 | bytes 54931456 | tf_op jit(solution)/shard_map/hqk,qhd->khd/dot_general | solution.py:291
  471.3 12.0 %fusion.49 = bf16[6,64,2048]{2,1,0:T(8,128)(2,1)S(1)} fusion(bf16[512,6,64]{0,2,1:T(8,128)(2,1)S(1)} %bitcast.248, f32[6,512,2048]{2,1,0:T(8,128)} %get-tuple-element.113, f32[6,512]{1,0:T(8,128)S(1)} %log_add_fusion, pred[512,2048]{1,0:T(8,128)(4,1)S(1)} %copy-done.34), kind=kOutput, calls=%fused_computation.61 | convolution fusion | flops 831258624 | bytes 28192768 | tf_op jit(solution)/shard_map/hqk,qhd->khd/dot_general | solution.py:284
  493.3 16.9 %concatenate.95 = f32[768,1664]{0,1:T(8,128)} concatenate(f32[768,384]{0,1:T(8,128)S(1)} %fusion.105, f32[768,384]{0,1:T(8,128)} %copy-done.32, f32[768,384]{0,1:T(8,128)} %get-tuple-element.117, f32[768,384]{0,1:T(8,128)} %fusion.111, f32[768,16]{0,1:T(8,128)S(1)} %fusion.163, f32[768,1]{0,1:T(1,128)S(1)} %broadcast_in_dim.199, f32[768,1]{0,1:T(1,128)S(1)} %broadcast_in_dim.200, ...), dimensions={1} | concatenate | bytes 10223616 | tf_op jit(solution)/shard_map/concatenate | solution.py:330
  544.8 7.2 %all-to-all-done.4 = bf16[16,24,1664]{2,1,0:T(8,128)(2,1)S(1)} async-done(((bf16[16,24,1664]{2,1,0:T(8,128)(2,1)}), bf16[16,24,1664]{2,1,0:T(8,128)(2,1)S(1)}, u32[]{:S(2)}, u32[]{:S(2)}) %all-to-all-start.4) | async-done | bytes 1277984 | tf_op jit(solution)/shard_map/all_to_all | solution.py:28
  576.4 56.1 %all-to-all-done.5 = bf16[16,24,1664]{2,1,0:T(8,128)(2,1)} async-done(((bf16[16,24,1664]{2,1,0:T(8,128)(2,1)}), bf16[16,24,1664]{2,1,0:T(8,128)(2,1)}, u32[]{:S(2)}, u32[]{:S(2)}) %all-to-all-start.5) | async-done | bytes 1277984 | tf_op jit(solution)/shard_map/all_to_all | solution.py:28
  657.9 22.7 %collective-permute-done.15 = f32[768,128]{0,1:T(8,128)} collective-permute-done((f32[768,128]{0,1:T(8,128)S(1)}, f32[768,128]{0,1:T(8,128)}, u32[]{:S(2)}, u32[]{:S(2)}) %collective-permute-start.15) | collective-permute-done | bytes 393248 | tf_op jit(solution)/shard_map/ppermute | solution.py:24
  (407 shorter events, 270.3 us)
Async XLA Ops:
  0.7 35.6 %collective-permute-start.1 = (bf16[512,768]{1,0:T(8,128)(2,1)}, bf16[512,768]{1,0:T(8,128)(2,1)}, u32[]{:S(2)}, u32[]{:S(2)}) collective-permute-start(bf16[512,768]{1,0:T(8,128)(2,1)} %param.17), channel_id=1, source_target_pairs={{0,4},{4,0},{1,5},{5,1},{2,6},{6,2},{3,7},{7,3},{8,12},{12,8},{9,1... | collective-permute-start | bytes 2359304 | tf_op jit(solution)/shard_map/ppermute | solution.py:24
  2.9 39.1 %collective-permute-start = (bf16[512,768]{1,0:T(8,128)(2,1)}, bf16[512,768]{1,0:T(8,128)(2,1)}, u32[]{:S(2)}, u32[]{:S(2)}) collective-permute-start(bf16[512,768]{1,0:T(8,128)(2,1)} %param.17), channel_id=1, source_target_pairs={{0,2},{2,0},{1,3},{3,1},{4,6},{6,4},{5,7},{7,5},{8,10},{10,8},{9,1... | collective-permute-start | bytes 2359304 | tf_op jit(solution)/shard_map/ppermute | solution.py:24
  7.3 96.4 %collective-permute-start.4 = (bf16[1,768,768]{1,2,0:T(8,128)(2,1)S(1)}, bf16[1,768,768]{1,2,0:T(8,128)(2,1)}, u32[]{:S(2)}, u32[]{:S(2)}) collective-permute-start(bf16[1,768,768]{1,2,0:T(8,128)(2,1)S(1)} %maximum_bitcast_fusion), channel_id=1, source_target_pairs={{0,1},{1,0},{2,3},{3,2},{4,5},{5,4},{6,7},{7,6},{8,9},{9,8},{10,11... | collective-permute-start | bytes 3538952 | tf_op jit(solution)/shard_map/ppermute | solution.py:24
  89.4 30.0 %collective-permute-start.3 = (bf16[512,768]{1,0:T(8,128)(2,1)}, bf16[512,768]{1,0:T(8,128)(2,1)}, u32[]{:S(2)}, u32[]{:S(2)}) collective-permute-start(bf16[512,768]{1,0:T(8,128)(2,1)} %convolution_convert_fusion.3), channel_id=1, source_target_pairs={{0,1},{1,0},{2,3},{3,2},{4,5},{5,4},{6,7},{7,6},{8,9},{9,8},{10,11... | collective-permute-start | bytes 2359304 | tf_op jit(solution)/shard_map/ppermute | solution.py:24
  91.6 44.1 %all-to-all-start.1 = ((bf16[16,40,896]{2,1,0:T(8,128)(2,1)}), bf16[16,40,896]{2,1,0:T(8,128)(2,1)}, u32[]{:S(2)}, u32[]{:S(2)}) async-start(bf16[16,40,896]{2,1,0:T(8,128)(2,1)} %bitcast.253), calls=%async_computation.1 | async-start | bytes 2293760 | tf_op jit(solution)/shard_map/all_to_all | solution.py:28
  106.7 69.5 %collective-permute-start.5 = (bf16[2,768,768]{1,2,0:T(8,128)(2,1)}, bf16[2,768,768]{1,2,0:T(8,128)(2,1)}, u32[]{:S(2)}, u32[]{:S(2)}) collective-permute-start(bf16[2,768,768]{1,2,0:T(8,128)(2,1)} %pad_maximum_fusion.4), channel_id=1, source_target_pairs={{0,4},{4,0},{1,5},{5,1},{2,6},{6,2},{3,7},{7,3},{8,12},{12,8},{9,1... | collective-permute-start | bytes 7077896 | tf_op jit(solution)/shard_map/ppermute | solution.py:24
  129.0 66.3 %collective-permute-start.16 = (bf16[384,2048]{1,0:T(8,128)(2,1)}, bf16[384,2048]{1,0:T(8,128)(2,1)}, u32[]{:S(2)}, u32[]{:S(2)}) collective-permute-start(bf16[384,2048]{1,0:T(8,128)(2,1)} %select_convert_fusion), channel_id=1, source_target_pairs={{0,2},{2,0},{1,3},{3,1},{4,6},{6,4},{5,7},{7,5},{8,10},{10,8},{9,1... | collective-permute-start | bytes 4718600 | tf_op jit(solution)/shard_map/ppermute | solution.py:24
  133.2 47.9 %collective-permute-start.19 = (bf16[512,768]{1,0:T(8,128)(2,1)}, bf16[512,768]{1,0:T(8,128)(2,1)}, u32[]{:S(2)}, u32[]{:S(2)}) collective-permute-start(bf16[512,768]{1,0:T(8,128)(2,1)} %select_convert_fusion.2), channel_id=1, source_target_pairs={{0,2},{2,0},{1,3},{3,1},{4,6},{6,4},{5,7},{7,5},{8,10},{10,8},{9,1... | collective-permute-start | bytes 2359304 | tf_op jit(solution)/shard_map/ppermute | solution.py:24
  135.7 47.7 %all-to-all-start = ((bf16[16,40,768]{2,1,0:T(8,128)(2,1)}), bf16[16,40,768]{2,1,0:T(8,128)(2,1)}, u32[]{:S(2)}, u32[]{:S(2)}) async-start(bf16[16,40,768]{2,1,0:T(8,128)(2,1)} %bitcast.255), calls=%async_computation | async-start | bytes 1966080 | tf_op jit(solution)/shard_map/all_to_all | solution.py:28
  180.1 93.8 %collective-permute-start.6 = (bf16[4,768,768]{1,2,0:T(8,128)(2,1)}, bf16[4,768,768]{1,2,0:T(8,128)(2,1)}, u32[]{:S(2)}, u32[]{:S(2)}) collective-permute-start(bf16[4,768,768]{1,2,0:T(8,128)(2,1)} %pad_maximum_fusion.2), channel_id=1, source_target_pairs={{0,2},{2,0},{1,3},{3,1},{4,6},{6,4},{5,7},{7,5},{8,10},{10,8},{9,1... | collective-permute-start | bytes 14155784 | tf_op jit(solution)/shard_map/ppermute | solution.py:24
  183.4 19.0 %all-to-all-start.8 = ((bf16[16,32,768]{2,1,0:T(8,128)(2,1)}), bf16[16,32,768]{2,1,0:T(8,128)(2,1)}, u32[]{:S(2)}, u32[]{:S(2)}) async-start(bf16[16,32,768]{2,1,0:T(8,128)(2,1)} %bitcast.242), calls=%async_computation.8 | async-start | bytes 1572864 | tf_op jit(solution)/shard_map/all_to_all | solution.py:28
  202.4 25.6 %all-to-all-start.6 = ((bf16[16,24,2048]{2,1,0:T(8,128)(2,1)}), bf16[16,24,2048]{2,1,0:T(8,128)(2,1)}, u32[]{:S(2)}, u32[]{:S(2)}) async-start(bf16[16,24,2048]{2,1,0:T(8,128)(2,1)} %bitcast.237), calls=%async_computation.6 | async-start | bytes 3145728 | tf_op jit(solution)/shard_map/all_to_all | solution.py:28
  228.9 14.9 %all-to-all-start.9 = ((bf16[16,32,768]{2,1,0:T(8,128)(2,1)}), bf16[16,32,768]{2,1,0:T(8,128)(2,1)}, u32[]{:S(2)}, u32[]{:S(2)}) async-start(bf16[16,32,768]{2,1,0:T(8,128)(2,1)} %broadcast_in_dim.204), calls=%async_computation.9 | async-start | bytes 1572864 | tf_op jit(solution)/shard_map/all_to_all | solution.py:28
  245.2 22.1 %all-to-all-start.7 = ((bf16[16,24,2048]{2,1,0:T(8,128)(2,1)}), bf16[16,24,2048]{2,1,0:T(8,128)(2,1)}, u32[]{:S(2)}, u32[]{:S(2)}) async-start(bf16[16,24,2048]{2,1,0:T(8,128)(2,1)} %broadcast_in_dim.203), calls=%async_computation.7 | async-start | bytes 3145728 | tf_op jit(solution)/shard_map/all_to_all | solution.py:28
  253.6 10.9 %collective-permute-start.21 = (bf16[512,768]{1,0:T(8,128)(2,1)}, bf16[512,768]{1,0:T(8,128)(2,1)}, u32[]{:S(2)}, u32[]{:S(2)}) collective-permute-start(bf16[512,768]{1,0:T(8,128)(2,1)} %bitcast.48), channel_id=1, source_target_pairs={{0,2},{2,0},{1,3},{3,1},{4,6},{6,4},{5,7},{7,5},{8,10},{10,8},{9,1... | collective-permute-start | bytes 2359304 | tf_op jit(solution)/shard_map/ppermute | solution.py:24
  267.3 264.8 %collective-permute-start.18 = (bf16[384,2048]{1,0:T(8,128)(2,1)}, bf16[384,2048]{1,0:T(8,128)(2,1)}, u32[]{:S(2)}, u32[]{:S(2)}) collective-permute-start(bf16[384,2048]{1,0:T(8,128)(2,1)} %bitcast.46), channel_id=1, source_target_pairs={{0,2},{2,0},{1,3},{3,1},{4,6},{6,4},{5,7},{7,5},{8,10},{10,8},{9,1... | collective-permute-start | bytes 4718600 | tf_op jit(solution)/shard_map/ppermute | solution.py:24
  297.8 24.7 %all-to-all-start.2 = ((bf16[16,40,768]{2,1,0:T(8,128)(2,1)}), bf16[16,40,768]{2,1,0:T(8,128)(2,1)S(1)}, u32[]{:S(2)}, u32[]{:S(2)}) async-start(bf16[16,40,768]{2,1,0:T(8,128)(2,1)} %bitcast.254), calls=%async_computation.2 | async-start | bytes 1966080 | tf_op jit(solution)/shard_map/all_to_all | solution.py:28
  322.6 26.9 %all-to-all-start.3 = ((bf16[16,40,896]{2,1,0:T(8,128)(2,1)}), bf16[16,40,896]{2,1,0:T(8,128)(2,1)}, u32[]{:S(2)}, u32[]{:S(2)}) async-start(bf16[16,40,896]{2,1,0:T(8,128)(2,1)} %pad_maximum_fusion.8), calls=%async_computation.3 | async-start | bytes 2293760 | tf_op jit(solution)/shard_map/all_to_all | solution.py:28
  344.8 38.7 %collective-permute-start.7 = (bf16[512,768]{1,0:T(8,128)(2,1)S(1)}, bf16[512,768]{1,0:T(8,128)(2,1)}, u32[]{:S(2)}, u32[]{:S(2)}) collective-permute-start(bf16[512,768]{1,0:T(8,128)(2,1)S(1)} %add_convert_fusion.7), channel_id=1, source_target_pairs={{0,1},{1,0},{2,3},{3,2},{4,5},{5,4},{6,7},{7,6},{8,9},{9,8},{10,11... | collective-permute-start | bytes 2359304 | tf_op jit(solution)/shard_map/ppermute | solution.py:24
  354.8 28.1 %collective-permute-start.8 = (bf16[512,768]{1,0:T(8,128)(2,1)S(1)}, bf16[512,768]{1,0:T(8,128)(2,1)S(1)}, u32[]{:S(2)}, u32[]{:S(2)}) collective-permute-start(bf16[512,768]{1,0:T(8,128)(2,1)S(1)} %fusion.88), channel_id=1, source_target_pairs={{0,1},{1,0},{2,3},{3,2},{4,5},{5,4},{6,7},{7,6},{8,9},{9,8},{10,11... | collective-permute-start | bytes 2359304 | tf_op jit(solution)/shard_map/ppermute | solution.py:24
  361.7 193.8 %collective-permute-start.22 = (bf16[4,768,768]{1,2,0:T(8,128)(2,1)}, bf16[4,768,768]{1,2,0:T(8,128)(2,1)}, u32[]{:S(2)}, u32[]{:S(2)}) collective-permute-start(bf16[4,768,768]{1,2,0:T(8,128)(2,1)} %slice.257), channel_id=1, source_target_pairs={{0,2},{2,0},{1,3},{3,1},{4,6},{6,4},{5,7},{7,5},{8,10},{10,8},{9,1... | collective-permute-start | bytes 14155784 | tf_op jit(solution)/shard_map/ppermute | solution.py:24
  513.1 11.1 %collective-permute-start.12 = (bf16[384,1664]{0,1:T(8,128)(2,1)S(1)}, bf16[384,1664]{0,1:T(8,128)(2,1)S(1)}, u32[]{:S(2)}, u32[]{:S(2)}) collective-permute-start(bf16[384,1664]{0,1:T(8,128)(2,1)S(1)} %select_convert_fusion.1), channel_id=1, source_target_pairs={{0,2},{2,0},{1,3},{3,1},{4,6},{6,4},{5,7},{7,5},{8,10},{10,8},{9,1... | collective-permute-start | bytes 3833864 | tf_op jit(solution)/shard_map/ppermute | solution.py:24
  521.5 16.1 %collective-permute-start.9 = (bf16[2,512,768]{2,1,0:T(8,128)(2,1)}, bf16[2,512,768]{2,1,0:T(8,128)(2,1)}, u32[]{:S(2)}, u32[]{:S(2)}) collective-permute-start(bf16[2,512,768]{2,1,0:T(8,128)(2,1)} %pad_maximum_fusion.7), channel_id=1, source_target_pairs={{0,2},{2,0},{1,3},{3,1},{4,6},{6,4},{5,7},{7,5},{8,10},{10,8},{9,1... | collective-permute-start | bytes 4718600 | tf_op jit(solution)/shard_map/ppermute | solution.py:24
  527.1 24.9 %all-to-all-start.4 = ((bf16[16,24,1664]{2,1,0:T(8,128)(2,1)}), bf16[16,24,1664]{2,1,0:T(8,128)(2,1)S(1)}, u32[]{:S(2)}, u32[]{:S(2)}) async-start(bf16[16,24,1664]{2,1,0:T(8,128)(2,1)} %bitcast.238), calls=%async_computation.4 | async-start | bytes 2555904 | tf_op jit(solution)/shard_map/all_to_all | solution.py:28
  543.4 25.4 %collective-permute-start.10 = (bf16[512,768]{1,0:T(8,128)(2,1)}, bf16[512,768]{1,0:T(8,128)(2,1)}, u32[]{:S(2)}, u32[]{:S(2)}) collective-permute-start(bf16[512,768]{1,0:T(8,128)(2,1)} %fusion.84), channel_id=1, source_target_pairs={{0,4},{4,0},{1,5},{5,1},{2,6},{6,2},{3,7},{7,3},{8,12},{12,8},{9,1... | collective-permute-start | bytes 2359304 | tf_op jit(solution)/shard_map/ppermute | solution.py:24
  552.2 10.2 %collective-permute-start.13 = (bf16[24,1664]{1,0:T(8,128)(2,1)S(1)}, bf16[24,1664]{1,0:T(8,128)(2,1)S(1)}, u32[]{:S(2)}, u32[]{:S(2)}) collective-permute-start(bf16[24,1664]{1,0:T(8,128)(2,1)S(1)} %reduce_sum.229), channel_id=1, source_target_pairs={{0,64},{64,0},{1,65},{65,1},{2,66},{66,2},{3,67},{67,3},{4,68},{68... | collective-permute-start | bytes 239624 | tf_op jit(solution)/shard_map/ppermute | solution.py:24
  562.1 78.1 %collective-permute-start.23 = (bf16[2,768,768]{1,2,0:T(8,128)(2,1)}, bf16[2,768,768]{1,2,0:T(8,128)(2,1)}, u32[]{:S(2)}, u32[]{:S(2)}) collective-permute-start(bf16[2,768,768]{1,2,0:T(8,128)(2,1)} %slice.259), channel_id=1, source_target_pairs={{0,4},{4,0},{1,5},{5,1},{2,6},{6,2},{3,7},{7,3},{8,12},{12,8},{9,1... | collective-permute-start | bytes 7077896 | tf_op jit(solution)/shard_map/ppermute | solution.py:24
  564.4 68.2 %all-to-all-start.5 = ((bf16[16,24,1664]{2,1,0:T(8,128)(2,1)}), bf16[16,24,1664]{2,1,0:T(8,128)(2,1)}, u32[]{:S(2)}, u32[]{:S(2)}) async-start(bf16[16,24,1664]{2,1,0:T(8,128)(2,1)} %broadcast_in_dim.202), calls=%async_computation.5 | async-start | bytes 2555904 | tf_op jit(solution)/shard_map/all_to_all | solution.py:28
  571.8 63.8 %collective-permute-start.11 = (bf16[512,768]{1,0:T(8,128)(2,1)S(1)}, bf16[512,768]{1,0:T(8,128)(2,1)}, u32[]{:S(2)}, u32[]{:S(2)}) collective-permute-start(bf16[512,768]{1,0:T(8,128)(2,1)S(1)} %fusion.87), channel_id=1, source_target_pairs={{0,1},{1,0},{2,3},{3,2},{4,5},{5,4},{6,7},{7,6},{8,9},{9,8},{10,11... | collective-permute-start | bytes 2359304 | tf_op jit(solution)/shard_map/ppermute | solution.py:24
  635.1 9.9 %collective-permute-start.14 = (bf16[384,1664]{0,1:T(8,128)(2,1)}, bf16[384,1664]{0,1:T(8,128)(2,1)S(1)}, u32[]{:S(2)}, u32[]{:S(2)}) collective-permute-start(bf16[384,1664]{0,1:T(8,128)(2,1)} %copy.109), channel_id=1, source_target_pairs={{0,2},{2,0},{1,3},{3,1},{4,6},{6,4},{5,7},{7,5},{8,10},{10,8},{9,1... | collective-permute-start | bytes 3833864 | tf_op jit(solution)/shard_map/ppermute | solution.py:24
  644.2 38.6 %collective-permute-start.24 = (bf16[768,768]{0,1:T(8,128)(2,1)}, bf16[768,768]{0,1:T(8,128)(2,1)}, u32[]{:S(2)}, u32[]{:S(2)}) collective-permute-start(bf16[768,768]{0,1:T(8,128)(2,1)} %slice_bitcast_fusion.2), channel_id=1, source_target_pairs={{0,1},{1,0},{2,3},{3,2},{4,5},{5,4},{6,7},{7,6},{8,9},{9,8},{10,11... | collective-permute-start | bytes 3538952 | tf_op jit(solution)/shard_map/ppermute | solution.py:24
  645.6 34.9 %collective-permute-start.15 = (f32[768,128]{0,1:T(8,128)S(1)}, f32[768,128]{0,1:T(8,128)}, u32[]{:S(2)}, u32[]{:S(2)}) collective-permute-start(f32[768,128]{0,1:T(8,128)S(1)} %maximum_convert_fusion.3), channel_id=1, source_target_pairs={{0,1},{1,0},{2,3},{3,2},{4,5},{5,4},{6,7},{7,6},{8,9},{9,8},{10,11... | collective-permute-start | bytes 1179656 | tf_op jit(solution)/shard_map/ppermute | solution.py:24
  (101 other events, 1064.1 us)
